TPU v7x, 32 devices: a whole 2x2x4 slice. The times are simulated.
32 devices in a mesh: ctx: 16 (over z, y, x), tp: 2 (over core).
Axes of the slice: x: 2, y: 2, z: 4, core: 2. Of those that a mesh axis runs over, the one named last changes fastest.
Arguments:
- inputs: bfloat16 [2048, 1024], P('ctx', 'tp'), may hold values from -6 to 6
- gate_in: bfloat16 [2048, 1024], P('ctx', 'tp'), may hold values from -6 to 6
- b_proj: bfloat16 [2048, 128], P('ctx'), may hold values from -0.5 to 0.5
- c_proj: bfloat16 [2048, 128], P('ctx'), may hold values from -0.5 to 0.5
- log_decay: float32 [8, 2048], P('tp', 'ctx'), may hold values from -0.75 to 0
- w_out: bfloat16 [1024, 4096], P('tp'), may hold values from -0.1875 to 0.1875
- cotangent: bfloat16 [2048, 4096], P(('ctx', 'tp')), may hold values from -6 to 6
Outputs:
- layer_out: bfloat16 [2048, 4096], P(('ctx', 'tp'))
- grad_inputs: bfloat16 [2048, 1024], P('ctx', 'tp')
- grad_gate: bfloat16 [2048, 1024], P('ctx', 'tp')
- grad_b: float32 [2048, 128], P(('ctx', 'tp'))
- grad_c: float32 [2048, 128], P(('ctx', 'tp'))
- grad_decay: float32 [8, 2048], P('tp', 'ctx')
All inputs are finite; a program needn't handle non-finite values.
Results may differ from a plain program's by a relative error of at most 0.017.
Values may be sent and summed in bfloat16 or wider, within the bound.
A program may use at most 128 MiB of HBM per device.

v0:
```python
import jax
import jax.numpy as jnp
from jax import lax
from jax.sharding import PartitionSpec as P

BLOCK = 128


def entering(shard, axis, combine, identity, reverse):
    count, place = (lax.axis_size(axis), lax.axis_index(axis))
    everything = jax.tree.map(lambda part: lax.all_gather(part, axis), shard)
    start = jax.tree.map(
        lambda part, zero: jnp.broadcast_to(jnp.asarray(zero, part.dtype), part.shape),
        shard,
        identity,
    )

    def lap(k, before):
        at = count - 1 - k if reverse else k
        reached = at > place if reverse else at < place
        new = combine(before, jax.tree.map(lambda part: part[at], everything))
        return jax.tree.map(lambda a, b: jnp.where(reached, a, b), new, before)

    return lax.fori_loop(0, count, lap, start)


def compose(earlier, later_part):
    return (earlier[0] * later_part[0], later_part[0][:, None, None] * earlier[1] + later_part[1])


def carried(block_decay, block_terms, backward):
    if backward:
        block_decay = jnp.flip(block_decay, 0)
        block_terms = jnp.flip(block_terms, 0)
    head_count = block_decay.shape[1]

    def local_step(running, packed):
        state_level, product = running
        decay_step, term_block = packed
        return (
            (decay_step[:, None, None] * state_level + term_block, decay_step * product),
            (state_level, product),
        )

    initial = (jnp.zeros(block_terms.shape[1:], jnp.float32), jnp.ones((head_count,), jnp.float32))
    (dev_state, dev_decay), (local_in, decay_before) = lax.scan(
        local_step, initial, (block_decay, block_terms)
    )
    identity = (jnp.ones((head_count,), jnp.float32), jnp.zeros(block_terms.shape[1:], jnp.float32))
    if backward:
        incoming = entering((dev_decay, dev_state), "ctx", compose, identity, True)[1]
    else:
        incoming = entering((dev_decay, dev_state), "ctx", compose, identity, False)[1]

    def resume(state_level, packed):
        decay_step, term_block = packed
        return (decay_step[:, None, None] * state_level + term_block, state_level)

    unused, states = lax.scan(resume, incoming, (block_decay, block_terms))
    if backward:
        states = jnp.flip(states, 0)
    return states


def local(inputs, gate_in, b_proj, c_proj, log_decay, w_out, cotangent):
    tok_rows, feature_width = inputs.shape
    head_count = log_decay.shape[0]
    head_dim = feature_width // head_count
    nblocks = tok_rows // BLOCK
    nstate = b_proj.shape[1]
    x_blocks = inputs.reshape(nblocks, BLOCK, head_count, head_dim)
    b_blocks = b_proj.reshape(nblocks, BLOCK, nstate)
    c_blocks = c_proj.reshape(nblocks, BLOCK, nstate)
    d_blocks = jnp.transpose(log_decay.reshape(head_count, nblocks, BLOCK), (1, 2, 0))
    gate_float = gate_in.astype(jnp.float32).reshape(nblocks, BLOCK, head_count, head_dim)
    sigmoid_z = jax.nn.sigmoid(gate_float)
    silu_z = gate_float * sigmoid_z
    position = jnp.arange(BLOCK)
    causal = position[:, None] >= position[None, :]
    lower_ones = causal.astype(jnp.float32)
    cumulative = jnp.einsum("qs,csh->cqh", lower_ones, d_blocks, precision=lax.Precision.HIGHEST)
    final_sum = cumulative[:, -1, :]
    block_decay = jnp.exp(final_sum)
    tail_weight = jnp.exp(final_sum[:, None, :] - cumulative)
    exp_cum = jnp.exp(cumulative)
    column_cum = jnp.transpose(cumulative, (0, 2, 1))
    differ = column_cum[:, :, :, None] - column_cum[:, :, None, :]
    decay_mat = jnp.where(causal, jnp.exp(jnp.minimum(differ, 0.0)), 0.0)
    scores = jnp.einsum("cqn,ckn->cqk", c_blocks, b_blocks, preferred_element_type=jnp.float32)
    mixing_b = (scores[:, None] * decay_mat).astype(jnp.bfloat16)
    y_intra = jnp.einsum("chqk,ckhp->cqhp", mixing_b, x_blocks, preferred_element_type=jnp.float32)
    weighted = (x_blocks.astype(jnp.float32) * tail_weight[..., None]).astype(jnp.bfloat16)
    block_state = jnp.einsum(
        "cqhp,cqn->chpn", weighted, b_blocks, preferred_element_type=jnp.float32
    )
    state_in = carried(block_decay, block_state, False)
    state_b = state_in.astype(jnp.bfloat16)
    y_inter = (
        jnp.einsum("cqn,chpn->cqhp", c_blocks, state_b, preferred_element_type=jnp.float32)
        * exp_cum[..., None]
    )
    y_full = y_intra + y_inter
    gated_out = (y_full * silu_z).astype(jnp.bfloat16).reshape(tok_rows, feature_width)
    layer_out = lax.psum_scatter(
        jnp.dot(gated_out, w_out, preferred_element_type=jnp.float32).astype(jnp.bfloat16),
        "tp",
        scatter_dimension=0,
        tiled=True,
    )
    state_in, state_b, y_inter, y_full, layer_out = (state_in, state_b, y_inter, y_full, layer_out)
    dgated = lax.dot_general(
        lax.all_gather(cotangent, "tp", axis=0, tiled=True),
        w_out,
        (((1,), (1,)), ((), ())),
        preferred_element_type=jnp.float32,
    )
    dgated = dgated.reshape(nblocks, BLOCK, head_count, head_dim)
    grad_y = dgated * silu_z
    grad_w = (grad_y * exp_cum[..., None]).astype(jnp.bfloat16)
    injected = jnp.einsum("cqhp,cqn->chpn", grad_w, c_blocks, preferred_element_type=jnp.float32)
    adjoint_next = carried(block_decay, injected, True)
    dgated, grad_y, grad_w, adjoint_next = (dgated, grad_y, grad_w, adjoint_next)
    grad_gate = (dgated * y_full * (sigmoid_z + gate_float * sigmoid_z * (1.0 - sigmoid_z))).astype(
        jnp.bfloat16
    )
    grad_gate = grad_gate.reshape(tok_rows, feature_width)
    grad_y_b = grad_y.astype(jnp.bfloat16)
    adjoint_b = adjoint_next.astype(jnp.bfloat16)
    pair_dots = jnp.einsum(
        "cqhp,ckhp->chqk", grad_y_b, x_blocks, preferred_element_type=jnp.float32
    )
    dmix = pair_dots * decay_mat
    dmix_b = dmix.astype(jnp.bfloat16)
    state_dx = (
        jnp.einsum("ckn,chpn->ckhp", b_blocks, adjoint_b, preferred_element_type=jnp.float32)
        * tail_weight[..., None]
    )
    grad_inputs = (
        jnp.einsum("chqk,cqhp->ckhp", mixing_b, grad_y_b, preferred_element_type=jnp.float32)
        + state_dx
    )
    grad_inputs = grad_inputs.astype(jnp.bfloat16).reshape(tok_rows, feature_width)
    b_terms = jnp.einsum("chqk,cqn->ckn", dmix_b, c_blocks, preferred_element_type=jnp.float32)
    b_terms = b_terms + jnp.einsum(
        "ckhp,chpn->ckn", weighted, adjoint_b, preferred_element_type=jnp.float32
    )
    c_terms = jnp.einsum("chqk,ckn->cqn", dmix_b, b_blocks, preferred_element_type=jnp.float32)
    c_terms = c_terms + jnp.einsum(
        "cqhp,chpn->cqn", grad_w, state_b, preferred_element_type=jnp.float32
    )
    grad_b, grad_c = (
        lax.psum_scatter(
            b_terms.reshape(tok_rows, nstate).astype(jnp.bfloat16),
            "tp",
            scatter_dimension=0,
            tiled=True,
        ).astype(jnp.float32),
        lax.psum_scatter(
            c_terms.reshape(tok_rows, nstate).astype(jnp.bfloat16),
            "tp",
            scatter_dimension=0,
            tiled=True,
        ).astype(jnp.float32),
    )
    cross_terms = dmix * scores[:, None]
    decay_flow = jnp.transpose(jnp.sum(cross_terms, 3) - jnp.sum(cross_terms, 2), (0, 2, 1))
    outflow = jnp.sum(x_blocks.astype(jnp.float32) * state_dx, 3)
    decay_flow = decay_flow + jnp.sum(grad_y * y_inter, 3) - outflow
    closing = jnp.sum(outflow, 1) + block_decay * jnp.sum(adjoint_next * state_in, (2, 3))
    decay_flow = decay_flow.at[:, -1, :].add(closing)
    grad_decay = jnp.einsum("ut,cuh->cth", lower_ones, decay_flow, precision=lax.Precision.HIGHEST)
    grad_decay = jnp.transpose(grad_decay, (2, 0, 1)).reshape(head_count, tok_rows)
    return (layer_out, grad_inputs, grad_gate, grad_b, grad_c, grad_decay)


def solution(mesh):
    in_specs = (
        P("ctx", "tp"),
        P("ctx", "tp"),
        P("ctx", None),
        P("ctx", None),
        P("tp", "ctx"),
        P("tp", None),
        P(("ctx", "tp"), None),
    )
    out_specs = (
        P(("ctx", "tp"), None),
        P("ctx", "tp"),
        P("ctx", "tp"),
        P(("ctx", "tp"), None),
        P(("ctx", "tp"), None),
        P("tp", "ctx"),
    )
    return jax.shard_map(local, mesh=mesh, in_specs=in_specs, out_specs=out_specs, check_vma=False)
```

profile of v0, /device:TPU:0, one launch (start us, length us, event | category | flops | bytes accessed | tf_op | source)
XLA Modules:
  0.0 223.7 jit_solution(1320845953040710723)
XLA Ops:
  8.0 0.8 fusion.29
  9.3 1.8 convolution_add_fusion.1
  11.4 10.0 %all-gather.7.cloned.1.call-done = bf16[128,4096]{1,0:T(8,128)(2,1)} async-done(((bf16[64,4096]{1,0:T(8,128)(2,1)}), bf16[128,4096]{1,0:T(8,128)(2,1)}) %all-gather.7.cloned.1.call-update) | async-done | bytes 1048592 | tf_op jit(solution)/shard_map/all_gather | solution.py:112
  21.3 4.0 %fusion.39 = f32[128,512]{1,0:T(8,128)S(1)} fusion(bf16[128,4096]{1,0:T(8,128)(2,1)} %all-gather.7.cloned.1.call-done, bf16[512,4096]{1,0:T(8,128)(2,1)} %param.18), kind=kOutput, calls=%fused_computation.77 | convolution fusion | flops 536870912 | bytes 5505024 | tf_op jit(solution)/shard_map/dot_general | solution.py:111
  25.5 0.9 convolution_add_fusion
  26.9 40.8 %all-gather = f32[16,1,4]{2,1,0:T(1,128)S(1)} all-gather(f32[1,1,4]{2,1,0:T(1,128)S(1)} %copy.56), channel_id=2, replica_groups=mesh['ctx'=16,'tp'=2] {'ctx'}, dimensions={0}, use_global_device_ids=true | all-gather | bytes 272 | tf_op jit(solution)/shard_map/all_gather | solution.py:11
  68.5 33.5 %all-gather.9.cloned.1.call-done = f32[64,128,128]{2,1,0:T(8,128)} async-done(((f32[4,128,128]{2,1,0:T(8,128)}), f32[64,128,128]{2,1,0:T(8,128)}) %all-gather.9.cloned.1.call-update) | async-done | bytes 4194320 | tf_op jit(solution)/shard_map/all_gather | solution.py:11
  102.0 17.5 %while.21 = (s32[]{:T(128)}, f32[4,128,128]{2,1,0:T(8,128)S(1)}, s32[]{:T(128)}, f32[16,4]{1,0:T(8,128)S(1)}, f32[16,4,128,128]{3,2,1,0:T(8,128)}, /*index=5*/s32[]{:T(128)}, s32[]{:T(128)}) while((s32[]{:T(128)}, f32[4,128,128]{2,1,0:T(8,128)S(1)}, s32[]{:T(128)}, f32[16,4]{1,0:T(8,128)S(1)}, f32[16,4,128,128]{3,2,1,0:T(8,128)}, ...), condition=%wide.region_1.2_spmd.clone, body=%wide.region_0.1_spmd.clone.sunk | while | flops 262148 | bytes 786585 | solution.py:24
  102.0 1.0 fusion.59
  103.1 1.1 fusion.59
  104.2 1.1 fusion.59
  105.3 1.1 fusion.59
  106.4 1.1 fusion.59
  107.5 1.1 fusion.59
  108.6 1.1 fusion.59
  109.7 1.1 fusion.59
  110.7 1.1 fusion.59
  111.9 1.1 fusion.59
  113.0 1.1 fusion.59
  114.0 1.1 fusion.59
  115.1 1.1 fusion.59
  116.2 1.1 fusion.59
  117.3 1.1 fusion.59
  118.4 1.1 fusion.59
  121.0 58.5 %all-gather.11.cloned.1.call-done = f32[64,128,128]{2,1,0:T(8,128)} async-done(((f32[4,128,128]{2,1,0:T(8,128)}), f32[64,128,128]{2,1,0:T(8,128)}) %all-gather.11.cloned.1.call-update) | async-done | bytes 4194320 | tf_op jit(solution)/shard_map/all_gather | solution.py:11
  179.5 17.7 %while.22 = (s32[]{:T(128)}, f32[4,128,128]{2,1,0:T(8,128)S(1)}, s32[]{:T(128)}, f32[16,4]{1,0:T(8,128)S(1)}, f32[16,4,128,128]{3,2,1,0:T(8,128)}, /*index=5*/s32[]{:T(128)}, s32[]{:T(128)}, s32[]{:T(128)}, s32[]{:T(128)}) while((s32[]{:T(128)}, f32[4,128,128]{2,1,0:T(8,128)S(1)}, s32[]{:T(128)}, f32[16,4]{1,0:T(8,128)S(1)}, ...), condition=%wide.region_4.5_spmd.clone, body=%wide.region_3.4_spmd.clone.sunk | while | flops 262152 | bytes 786647 | solution.py:24
  179.5 1.0 fusion.60
  180.6 1.1 fusion.60
  181.7 1.1 fusion.60
  182.8 1.1 fusion.60
  183.9 1.1 fusion.60
  185.0 1.1 fusion.60
  186.1 1.1 fusion.60
  187.3 1.1 fusion.60
  188.4 1.1 fusion.60
  189.5 1.1 fusion.60
  190.6 1.1 fusion.60
  191.7 1.1 fusion.60
  192.8 1.1 fusion.60
  193.9 1.1 fusion.60
  195.0 1.1 fusion.60
  196.1 1.1 fusion.60
  197.4 0.8 fusion.7
  198.2 3.9 %convolution_convert_fusion = bf16[128,4096]{1,0:T(8,128)(2,1)} fusion(bf16[128,512]{0,1:T(8,128)(2,1)S(1)} %bitcast.161, bf16[512,4096]{1,0:T(8,128)(2,1)} %param.18), kind=kOutput, calls=%fused_computation.6 | convolution fusion | flops 537395200 | bytes 5373952 | tf_op jit(solution)/shard_map/dot_general | solution.py:105
  203.0 1.3 convert_element_type.112
  205.3 0.8 copy.75
  207.0 1.3 convert_element_type.110
  208.3 8.5 %reduce-scatter.4.cloned.1.call-done = bf16[64,4096]{1,0:T(8,128)(2,1)} async-done(((bf16[128,4096]{1,0:T(8,128)(2,1)}), bf16[64,4096]{1,0:T(8,128)(2,1)}) %reduce-scatter.4.cloned.1.call-update) | async-done | bytes 524304 | tf_op jit(solution)/shard_map/reduce_scatter | solution.py:104
  (88 shorter events, 7.5 us)
Async XLA Ops:
  7.2 2.1 copy-start
  7.2 18.2 %copy-start.2 = (bf16[128,512]{1,0:T(8,128)(2,1)S(1)}, bf16[128,512]{1,0:T(8,128)(2,1)}, u32[]{:S(2)}) copy-start(bf16[128,512]{1,0:T(8,128)(2,1)} %param.14) | copy-start | bytes 393220
  7.2 14.1 %all-gather.7.cloned.1.call-start = ((), (), s32[]{:S(2)}) async-start(), calls=%async_computation.4 | async-start | bytes 1572864 | tf_op jit(solution)/shard_map/all_gather | solution.py:112
  7.9 94.1 %all-gather.9.cloned.1.call-start = ((), (), s32[]{:S(2)}) async-start(), calls=%async_computation.7 | async-start | bytes 4456448 | tf_op jit(solution)/shard_map/all_gather | solution.py:11
  9.1 16.4 %copy-start.3 = (bf16[128,128]{1,0:T(8,128)(2,1)S(1)}, bf16[128,128]{1,0:T(8,128)(2,1)}, u32[]{:S(2)}) copy-start(bf16[128,128]{1,0:T(8,128)(2,1)} %param.16) | copy-start | bytes 98308
  11.1 15.4 %copy-start.1 = (bf16[128,512]{1,0:T(8,128)(2,1)S(1)}, bf16[128,512]{1,0:T(8,128)(2,1)}, u32[]{:S(2)}) copy-start(bf16[128,512]{1,0:T(8,128)(2,1)} %param.13) | copy-start | bytes 393220
  11.2 168.3 %all-gather.11.cloned.1.call-start = ((), (), s32[]{:S(2)}) async-start(), calls=%async_computation.8 | async-start | bytes 4456448 | tf_op jit(solution)/shard_map/all_gather | solution.py:11
  26.5 176.5 %reduce-scatter.8.cloned.1.call-start = ((), (), s32[]{:S(2)}) async-start(), calls=%async_computation.6 | async-start | bytes 49152 | tf_op jit(solution)/shard_map/reduce_scatter | solution.py:158
  120.7 86.3 %reduce-scatter.6.cloned.1.call-start = ((), (), s32[]{:S(2)}) async-start(), calls=%async_computation.5 | async-start | bytes 49152 | tf_op jit(solution)/shard_map/reduce_scatter | solution.py:152
  198.2 18.6 %reduce-scatter.4.cloned.1.call-start = ((), (), s32[]{:S(2)}) async-start(), calls=%async_computation.3 | async-start | bytes 1572864 | tf_op jit(solution)/shard_map/reduce_scatter | solution.py:104
Sparse Core Ops, SparseCore 0:
  9.6 11.7 all-gather.6
  24.7 77.2 all-gather.8
  104.8 74.6 all-gather.10
  182.1 6.0 reduce-scatter.7
  198.3 6.0 reduce-scatter.5
  207.1 9.7 reduce-scatter.3
where the time goes:
time: 225 us; the launch traced here: 224 us
  waiting for transfers between devices  111 us (49%)
  blocking collectives  40.8 us (18%)
  other arithmetic  36.8 us (16%)
  matrix products  15.8 us (7%)
  between operations  14.3 us (6%)
  local copies, waits for them, and re-layouts  3.34 us (1%)
    all_gather x2, waiting for transfers between devices, entering(): everything = jax.tree.map(lambda part: lax.all_gather(part, axis), shard)  92 us
    all_gather x1, blocking collectives, entering(): everything = jax.tree.map(lambda part: lax.all_gather(part, axis), shard)  40.8 us
    select_n x32, other arithmetic, lap(): return jax.tree.map(lambda a, b: jnp.where(reached, a, b), new, before)  33.7 us
    all_gather x1, waiting for transfers between devices, local(): lax.all_gather(cotangent, 'tp', axis=0, tiled=True)  9.96 us
    reduce_scatter x1, waiting for transfers between devices, local(): lax.psum_scatter(jnp.dot(gated_out, w_out, preferred_element_type=jnp.flo...  8.52 us
  transfers between devices with their start and end apart: 6, of which 4 were waited for; matrix products, arithmetic and copies ran while one was open for 25% of the time, Pallas kernels for 0%

commit v1 on v0

v1 whole, which is shorter than its diff:
```python
import functools

import jax
import jax.numpy as jnp
from jax import lax
from jax.experimental import pallas as pl
from jax.experimental.pallas import tpu as pltpu
from jax.sharding import PartitionSpec as P

BLOCK = 128
MESH = pl.DeviceIdType.MESH
F32, BF16 = jnp.float32, jnp.bfloat16
EXTRA = 16


def mm(a, b):
    return jnp.dot(a, b, preferred_element_type=F32)


def mm_nt(a, b, precision=None):
    return lax.dot_general(
        a, b, (((1,), (1,)), ((), ())), preferred_element_type=F32, precision=precision
    )


def mm_tn(a, b):
    return lax.dot_general(a, b, (((0,), (0,)), ((), ())), preferred_element_type=F32)


def two_parts(a):
    high = a.astype(BF16).astype(F32)
    shape = (EXTRA // 2, a.shape[1])
    rows = [jnp.broadcast_to(high, shape), jnp.broadcast_to(a - high, shape)]
    return jnp.concatenate(rows, axis=0).astype(BF16)


def kernel(
    sizes,
    x_hbm, g_hbm, b_hbm, c_hbm, ld_ref, w_hbm, cot_hbm,
    lo_out, gx_out, gg_out, gb_out, gc_out, gd_out,
    x_v, g_v, b_v, c_v, w_v, cot_v,
    cb_v, tail_v, expc_v, mask_v, wt_v, mix_v, sil_v, dsil_v, dg_v, gy_v, gyb_v, gw_v, y_v,
    gated_v, dmix_v, cross_v, yint_v, flow_v,
    msg1, rec1, loc, msg2, rec2, ent, msg3, st,
    lo_part, lo_rec, bc_part, bc_rec,
    lsem, cs, cr, s1s, s1r, s2s, s2r, s3s, s3r, ls, lr, bs, br,
):
    inner, outer, n_tp, w_chunks, lo_chunks = sizes
    heads = ld_ref.shape[0]
    width = x_v.shape[1]
    dim = width // heads
    nstate = b_v.shape[1]
    depth = w_v.shape[1]
    rows = cot_hbm.shape[0]
    part = width // inner
    place, tp = lax.axis_index("ctx"), lax.axis_index("tp")
    ip, zq = lax.rem(place, inner), lax.div(place, inner)
    mine = pl.multiple_of(tp * rows, rows)

    def lanes(h):
        return slice(h * dim, (h + 1) * dim)

    loads = [(x_hbm, x_v), (b_hbm, b_v), (c_hbm, c_v), (g_hbm, g_v)]
    loads.append((cot_hbm, cot_v.at[pl.ds(mine, rows)]))
    wrows = width // w_chunks
    for k in range(w_chunks):
        cut = pl.ds(k * wrows, wrows)
        loads.append((w_hbm.at[cut], w_v.at[cut]))
    loads = [pltpu.make_async_copy(s, d, lsem.at[i]) for i, (s, d) in enumerate(loads)]
    for copy in loads:
        copy.start()

    def plane(d):
        to = lax.rem(ip + d, inner)
        return to, (zq * inner + to, tp)

    def other(d):
        to = lax.rem(tp + d, n_tp)
        return to, (place, to)

    barrier = pltpu.get_barrier_semaphore()
    for d in range(1, n_tp):
        pl.semaphore_signal(barrier, inc=1, device_id=other(d)[1], device_id_type=MESH)
    for d in range(1, inner):
        pl.semaphore_signal(barrier, inc=1, device_id=plane(d)[1], device_id_type=MESH)
    for d in range(1, outer):
        to = lax.rem(zq + d, outer) * inner + ip
        pl.semaphore_signal(barrier, inc=1, device_id=(to, tp), device_id_type=MESH)
    pl.semaphore_wait(barrier, n_tp + inner + outer - 3)

    def remote(src, dst, ssem, rsem, device):
        return pltpu.make_async_remote_copy(
            src_ref=src, dst_ref=dst, send_sem=ssem, recv_sem=rsem,
            device_id=device, device_id_type=MESH,
        )

    cot_copies = [
        remote(cot_hbm, cot_v.at[pl.ds(mine, rows)], cs.at[d], cr.at[d], other(d)[1])
        for d in range(1, n_tp)
    ]
    for copy in cot_copies:
        copy.start()

    sends1, sends3 = {0: [], 1: []}, {0: [], 1: []}

    def start_plane(k, total, decays):
        for i in range(inner):
            msg1[k, i, 0:part, :] = total[i * part:(i + 1) * part].astype(BF16)
            msg1[k, i, part:part + EXTRA, :] = two_parts(decays[i * part // dim])
        for d in range(1, inner):
            to, device = plane(d)
            copy = remote(msg1.at[k, to], rec1.at[k, ip], s1s.at[k, d], s1r.at[k, d], device)
            copy.start()
            sends1[k].append(copy)
        rec1[k, pl.ds(ip, 1)] = msg1[k, pl.ds(ip, 1)]

    def z_copy(k, d):
        to = zq + d if k == 0 else zq - d
        return remote(
            msg2.at[k], rec2.at[k, zq], s2s.at[k, d], s2r.at[k, d], (to * inner + ip, tp)
        )

    def ahead(k, d):
        return zq + d < outer if k == 0 else zq - d >= 0

    def behind(k, d):
        return zq - d >= 0 if k == 0 else zq + d < outer

    def plane_scan(k):
        for copy in sends1[k]:
            copy.wait_recv()
        before = {}
        state = jnp.zeros((part, nstate), F32)
        decay = jnp.ones((1, nstate), F32)
        for p in range(inner) if k == 0 else reversed(range(inner)):
            loc[k, p] = state
            before[p] = decay
            own = rec1[k, p].astype(F32)
            step = own[part:part + 1] + own[part + EXTRA // 2:part + EXTRA // 2 + 1]
            state = step * state + own[0:part]
            decay = decay * step
        msg2[k, 0:part, :] = state.astype(BF16)
        msg2[k, part:part + EXTRA, :] = two_parts(decay)
        for d in range(1, outer):
            @pl.when(ahead(k, d))
            def _():
                z_copy(k, d).start()
        return before

    def z_scan(k, before):
        ent[k] = jnp.zeros((part, nstate), F32)
        for d in reversed(range(1, outer)):
            @pl.when(behind(k, d))
            def _():
                z_copy(k, d).wait_recv()
                own = rec2[k, zq - d if k == 0 else zq + d].astype(F32)
                step = own[part:part + 1] + own[part + EXTRA // 2:part + EXTRA // 2 + 1]
                ent[k] = step * ent[k] + own[0:part]
        entering = ent[k]
        for p in range(inner):
            msg3[k, p] = (before[p] * entering + loc[k, p]).astype(BF16)
        slot = pl.ds(pl.multiple_of(ip * part, part), part)
        for d in range(1, inner):
            to, device = plane(d)
            copy = remote(msg3.at[k, to], st.at[k, slot], s3s.at[k, d], s3r.at[k, d], device)
            copy.start()
            sends3[k].append(copy)
        st[k, slot, :] = msg3[k, pl.ds(ip, 1)].reshape(part, nstate)

    t_at = lax.broadcasted_iota(jnp.int32, (BLOCK, BLOCK), 0)
    s_at = lax.broadcasted_iota(jnp.int32, (BLOCK, BLOCK), 1)
    causal = t_at >= s_at
    lower = causal.astype(F32)
    steps = ld_ref[...]
    if heads % 8:
        steps = jnp.concatenate([steps, jnp.zeros((8 - heads % 8, BLOCK), F32)], axis=0)
    cum = mm_nt(steps, lower, lax.Precision.HIGHEST)
    decays = []
    loads[0].wait()
    loads[1].wait()
    for h in range(heads):
        column = jnp.transpose(jnp.broadcast_to(cum[h:h + 1], (BLOCK, BLOCK)))
        end = cum[h:h + 1, BLOCK - 1:BLOCK]
        tail = jnp.exp(end - column)
        cb_v[h] = column
        tail_v[h] = tail
        decays.append(jnp.broadcast_to(jnp.exp(end), (1, nstate)))
        wt_v[:, lanes(h)] = (x_v[:, lanes(h)].astype(F32) * tail).astype(BF16)
    start_plane(0, mm_tn(wt_v[...], b_v[...]), decays)

    loads[2].wait()
    loads[3].wait()
    for h in range(heads):
        expc_v[h] = jnp.exp(cb_v[h])
        v = g_v[:, lanes(h)].astype(F32)
        sig = 1.0 / (1.0 + jnp.exp(-v))
        sil_v[:, lanes(h)] = v * sig
        dsil_v[:, lanes(h)] = sig + v * sig * (1.0 - sig)
    scores = mm_nt(c_v[...], b_v[...])

    loads[4].wait()
    for copy in cot_copies:
        copy.wait_recv()
    before_f = None
    for k in range(w_chunks):
        loads[5 + k].wait()
        cut = slice(k * wrows, (k + 1) * wrows)
        dg_v[:, cut] = mm_nt(cot_v[...], w_v[cut, :])
        if k == 0:
            before_f = plane_scan(0)
    for h in range(heads):
        gy = dg_v[:, lanes(h)] * sil_v[:, lanes(h)]
        gy_v[:, lanes(h)] = gy
        gyb_v[:, lanes(h)] = gy.astype(BF16)
        gw_v[:, lanes(h)] = (gy * expc_v[h]).astype(BF16)
    start_plane(1, mm_tn(gw_v[...], c_v[...]), decays)

    for h in range(heads):
        column = cb_v[h]
        differ = column - jnp.broadcast_to(cum[h:h + 1], (BLOCK, BLOCK))
        mask = jnp.where(causal, jnp.exp(jnp.minimum(differ, 0.0)), 0.0)
        mask_v[h] = mask
        mix = (scores * mask).astype(BF16)
        mix_v[h] = mix
        y_v[:, lanes(h)] = mm(mix, x_v[:, lanes(h)])
    z_scan(0, before_f)
    before_b = plane_scan(1)

    total = jnp.zeros((BLOCK, BLOCK), F32)
    for h in range(heads):
        dmix = mm_nt(gyb_v[:, lanes(h)], x_v[:, lanes(h)]) * mask_v[h]
        total = total + dmix
        cross_v[h] = dmix * scores
    dmix_v[...] = total.astype(BF16)
    z_scan(1, before_b)

    for copy in sends3[0]:
        copy.wait_recv()
    y_inter = mm_nt(c_v[...], st[0])
    for h in range(heads):
        inter = y_inter[:, lanes(h)] * expc_v[h]
        yint_v[:, lanes(h)] = inter
        y = y_v[:, lanes(h)] + inter
        gated_v[:, lanes(h)] = (y * sil_v[:, lanes(h)]).astype(BF16)
        gg_out[:, lanes(h)] = (dg_v[:, lanes(h)] * y * dsil_v[:, lanes(h)]).astype(BF16)
    lcols = depth // lo_chunks
    lo_copies = []
    for k in range(lo_chunks):
        cut = slice(k * lcols, (k + 1) * lcols)
        lo_part[:, cut] = mm(gated_v[...], w_v[:, cut]).astype(BF16)
        for d in range(1, n_tp):
            to, device = other(d)
            theirs = pl.ds(pl.multiple_of(to * rows, rows), rows)
            copy = remote(
                lo_part.at[theirs, pl.ds(k * lcols, lcols)],
                lo_rec.at[d - 1, :, pl.ds(k * lcols, lcols)],
                ls.at[k, d], lr.at[k, d], device,
            )
            copy.start()
            lo_copies.append((k, d, copy))

    for copy in sends3[1]:
        copy.wait_recv()
    adj = st[1]
    bc_part[:, 0:nstate] = (mm_tn(dmix_v[...], c_v[...]) + mm(wt_v[...], adj)).astype(BF16)
    bc_part[:, nstate:2 * nstate] = (
        mm(dmix_v[...], b_v[...]) + mm(gw_v[...], st[0])
    ).astype(BF16)
    bc_copies = []
    for d in range(1, n_tp):
        to, device = other(d)
        theirs = pl.ds(pl.multiple_of(to * rows, rows), rows)
        copy = remote(bc_part.at[theirs], bc_rec.at[d - 1], bs.at[d], br.at[d], device)
        copy.start()
        bc_copies.append(copy)
    dx = mm_nt(b_v[...], adj)
    flow_v[...] = jnp.zeros(flow_v.shape, F32)
    last = lax.broadcasted_iota(jnp.int32, (1, BLOCK), 1) == BLOCK - 1
    for h in range(heads):
        state_dx = dx[:, lanes(h)] * tail_v[h]
        grad = mm_tn(mix_v[h], gyb_v[:, lanes(h)]) + state_dx
        gx_out[:, lanes(h)] = grad.astype(BF16)
        outflow = x_v[:, lanes(h)].astype(F32) * state_dx
        cross = cross_v[h]
        by_row = cross + gy_v[:, lanes(h)] * yint_v[:, lanes(h)] - outflow
        flow = jnp.sum(jnp.transpose(by_row) - cross, axis=0, keepdims=True)
        held = st[0, lanes(h), :].astype(F32) * st[1, lanes(h), :].astype(F32)
        closing = jnp.sum(outflow + decays[h] * held, axis=0, keepdims=True)
        closing = jnp.sum(closing, axis=1, keepdims=True)
        flow_v[h:h + 1, :] = flow + jnp.where(last, closing, 0.0)
    grad_decay = lax.dot_general(
        flow_v[...], lower, (((1,), (0,)), ((), ())),
        preferred_element_type=F32, precision=lax.Precision.HIGHEST,
    )
    gd_out[...] = grad_decay[0:heads]

    for k in range(lo_chunks):
        cut = slice(k * lcols, (k + 1) * lcols)
        out = lo_part[pl.ds(mine, rows), cut].astype(F32)
        for at, d, copy in lo_copies:
            if at == k:
                copy.wait_recv()
                out = out + lo_rec[d - 1, :, cut].astype(F32)
        lo_out[:, cut] = out.astype(BF16)
    both = bc_part[pl.ds(mine, rows), :].astype(F32)
    for d, copy in enumerate(bc_copies):
        copy.wait_recv()
        both = both + bc_rec[d].astype(F32)
    gb_out[...] = both[:, 0:nstate]
    gc_out[...] = both[:, nstate:2 * nstate]

    for copy in cot_copies + sends1[0] + sends1[1] + sends3[0] + sends3[1] + bc_copies:
        copy.wait_send()
    for _, _, copy in lo_copies:
        copy.wait_send()
    for k in range(2):
        for d in range(1, outer):
            @pl.when(ahead(k, d))
            def _():
                z_copy(k, d).wait_send()


def local(n_ctx, n_tp, inputs, gate_in, b_proj, c_proj, log_decay, w_out, cotangent):
    tok, width = inputs.shape
    heads = log_decay.shape[0]
    dim = width // heads
    nstate = b_proj.shape[1]
    rows, depth = cotangent.shape
    inner = 1
    while (2 * inner) ** 2 <= n_ctx and n_ctx % (2 * inner) == 0:
        inner *= 2
    inner = max(inner, min(heads, n_ctx))
    outer = n_ctx // inner
    part = width // inner
    assert tok == BLOCK and dim == BLOCK and nstate == BLOCK and dim % part == 0
    w_chunks, lo_chunks = 2, 4
    square = (heads, BLOCK, BLOCK)
    wide = (BLOCK, width)
    dma = pltpu.SemaphoreType.DMA
    scratch = [
        pltpu.VMEM(wide, BF16),
        pltpu.VMEM(wide, BF16),
        pltpu.VMEM((BLOCK, nstate), BF16),
        pltpu.VMEM((BLOCK, nstate), BF16),
        pltpu.VMEM((width, depth), BF16),
        pltpu.VMEM((BLOCK, depth), BF16),
        pltpu.VMEM(square, F32),
        pltpu.VMEM(square, F32),
        pltpu.VMEM(square, F32),
        pltpu.VMEM(square, F32),
        pltpu.VMEM(wide, BF16),
        pltpu.VMEM(square, BF16),
        pltpu.VMEM(wide, F32),
        pltpu.VMEM(wide, F32),
        pltpu.VMEM(wide, F32),
        pltpu.VMEM(wide, F32),
        pltpu.VMEM(wide, BF16),
        pltpu.VMEM(wide, BF16),
        pltpu.VMEM(wide, F32),
        pltpu.VMEM(wide, BF16),
        pltpu.VMEM((BLOCK, BLOCK), BF16),
        pltpu.VMEM(square, F32),
        pltpu.VMEM(wide, F32),
        pltpu.VMEM((-(-heads // 8) * 8, BLOCK), F32),
        pltpu.VMEM((2, inner, part + EXTRA, nstate), BF16),
        pltpu.VMEM((2, inner, part + EXTRA, nstate), BF16),
        pltpu.VMEM((2, inner, part, nstate), F32),
        pltpu.VMEM((2, part + EXTRA, nstate), BF16),
        pltpu.VMEM((2, outer, part + EXTRA, nstate), BF16),
        pltpu.VMEM((2, part, nstate), F32),
        pltpu.VMEM((2, inner, part, nstate), BF16),
        pltpu.VMEM((2, width, nstate), BF16),
        pltpu.VMEM((BLOCK, depth), BF16),
        pltpu.VMEM((max(n_tp - 1, 1), rows, depth), BF16),
        pltpu.VMEM((BLOCK, 2 * nstate), BF16),
        pltpu.VMEM((max(n_tp - 1, 1), rows, 2 * nstate), BF16),
        dma((5 + w_chunks,)),
        dma((n_tp,)), dma((n_tp,)),
        dma((2, inner)), dma((2, inner)),
        dma((2, outer)), dma((2, outer)),
        dma((2, inner)), dma((2, inner)),
        dma((lo_chunks, n_tp)), dma((lo_chunks, n_tp)),
        dma((n_tp,)), dma((n_tp,)),
    ]
    anywhere = pl.BlockSpec(memory_space=pl.ANY)
    vmem = pl.BlockSpec(memory_space=pltpu.VMEM)
    shape = jax.ShapeDtypeStruct
    return pl.pallas_call(
        functools.partial(kernel, (inner, outer, n_tp, w_chunks, lo_chunks)),
        out_shape=(
            shape((rows, depth), BF16),
            shape(wide, BF16),
            shape(wide, BF16),
            shape((rows, nstate), F32),
            shape((rows, nstate), F32),
            shape((heads, BLOCK), F32),
        ),
        in_specs=[anywhere] * 4 + [vmem] + [anywhere] * 2,
        out_specs=(vmem,) * 6,
        scratch_shapes=scratch,
        compiler_params=pltpu.CompilerParams(
            collective_id=0, has_side_effects=True, vmem_limit_bytes=40 * 1024 * 1024
        ),
        cost_estimate=pl.CostEstimate(
            flops=4 * BLOCK * width * depth, bytes_accessed=8 * 1024 * 1024, transcendentals=0
        ),
    )(inputs, gate_in, b_proj, c_proj, log_decay, w_out, cotangent)


def solution(mesh):
    in_specs = (
        P("ctx", "tp"),
        P("ctx", "tp"),
        P("ctx", None),
        P("ctx", None),
        P("tp", "ctx"),
        P("tp", None),
        P(("ctx", "tp"), None),
    )
    out_specs = (
        P(("ctx", "tp"), None),
        P("ctx", "tp"),
        P("ctx", "tp"),
        P(("ctx", "tp"), None),
        P(("ctx", "tp"), None),
        P("tp", "ctx"),
    )
    body = functools.partial(local, mesh.shape["ctx"], mesh.shape["tp"])
    return jax.shard_map(body, mesh=mesh, in_specs=in_specs, out_specs=out_specs, check_vma=False)
```

time: 225 us -> 37.8 us (0.17)
  waiting for transfers between devices: 111 us -> 0 us
  blocking collectives: 40.8 us -> 0 us
  other arithmetic: 36.8 us -> 0 us
  Pallas kernels: 0 us -> 25.6 us
  matrix products: 15.8 us -> 0 us
  between operations: 14.3 us -> 0.66 us
  local copies, waits for them, and re-layouts: 3.34 us -> 11.1 us
    all_gather x3 -> x0, waiting for transfers between devices: 102 us -> none  [the longest x2 92 us: entering(): everything = jax.tree.map(lambda part: lax.all_gather(part, axis), shard)]
    all_gather x1 -> x0, blocking collectives: 40.8 us -> none  [entering(): everything = jax.tree.map(lambda part: lax.all_gather(part, axis), shard)]
    select_n x32 -> x0, other arithmetic: 33.7 us -> none  [lap(): return jax.tree.map(lambda a, b: jnp.where(reached, a, b), new, before)]
    pallas_call x0 -> x1, Pallas kernels: none -> 25.6 us  [local(): pl.pallas_call(functools.partial(kernel, (inner, outer, n_tp, w_chunks, l...]
    dot_general x16 -> x0, matrix products: 15.8 us -> none  [the longest x1 4.04 us: local(): lax.dot_general(lax.all_gather(cotangent, 'tp', axis=0, tiled=True), w_ou...]
    unnamed x12 -> x20, local copies, waits for them, and re-layouts: 1.77 us -> 11.1 us
    reduce_scatter x3 -> x0, waiting for transfers between devices: 8.53 us -> none  [the longest x1 8.52 us: local(): lax.psum_scatter(jnp.dot(gated_out, w_out, preferred_element_type=jnp.flo...]
    convert_element_type x2 -> x0, other arithmetic: 2.67 us -> none  [local(): grad_b, grad_c = (lax.psum_scatter(b_terms.reshape(tok_rows, nstate).asty...]
  transfers between devices with their start and end apart: 6 -> 0, of which waited for: 4 -> 0; matrix products, arithmetic and copies ran while one was open for 25% -> 0% of each run, Pallas kernels for 0% -> 0%
where the time goes in v1:
time: 37.8 us; the launch traced here: 37.4 us
  Pallas kernels  25.6 us (68%)
  local copies, waits for them, and re-layouts  11.1 us (29%)
  between operations  0.66 us (2%)
    pallas_call x1, Pallas kernels, local(): pl.pallas_call(functools.partial(kernel, (inner, outer, n_tp, w_chunks, l...  25.6 us
    unnamed x20, local copies, waits for them, and re-layouts  11.1 us

profile of v1, /device:TPU:0, one launch (start us, length us, event | category | flops | bytes accessed | tf_op | source)
XLA Modules:
  0.0 37.4 jit_solution(7853762057011552028)
XLA Ops:
  0.6 0.0 copy-start
  0.6 2.2 %copy-done = bf16[512,4096]{1,0:T(8,128)(2,1)S(1)} copy-done((bf16[512,4096]{1,0:T(8,128)(2,1)S(1)}, bf16[512,4096]{1,0:T(8,128)(2,1)}, u32[]{:S(2)}) %copy-start) | copy-done | bytes 4194328
  2.8 0.0 copy-start.1
  2.8 1.0 %copy-done.1 = bf16[64,4096]{1,0:T(8,128)(2,1)S(1)} copy-done((bf16[64,4096]{1,0:T(8,128)(2,1)S(1)}, bf16[64,4096]{1,0:T(8,128)(2,1)}, u32[]{:S(2)}) %copy-start.1) | copy-done | bytes 524312
  3.9 0.0 copy-start.2
  3.9 0.9 %copy-done.2 = bf16[128,512]{1,0:T(8,128)(2,1)S(1)} copy-done((bf16[128,512]{1,0:T(8,128)(2,1)S(1)}, bf16[128,512]{1,0:T(8,128)(2,1)}, u32[]{:S(2)}) %copy-start.2) | copy-done | bytes 131096
  4.8 0.0 copy-start.3
  4.8 0.9 %copy-done.3 = bf16[128,512]{1,0:T(8,128)(2,1)S(1)} copy-done((bf16[128,512]{1,0:T(8,128)(2,1)S(1)}, bf16[128,512]{1,0:T(8,128)(2,1)}, u32[]{:S(2)}) %copy-start.3) | copy-done | bytes 131096
  5.7 0.0 copy-start.4
  5.7 0.8 %copy-done.4 = bf16[128,128]{1,0:T(8,128)(2,1)S(1)} copy-done((bf16[128,128]{1,0:T(8,128)(2,1)S(1)}, bf16[128,128]{1,0:T(8,128)(2,1)}, u32[]{:S(2)}) %copy-start.4) | copy-done | bytes 32792
  6.4 0.0 copy-start.5
  6.4 0.8 %copy-done.5 = bf16[128,128]{1,0:T(8,128)(2,1)S(1)} copy-done((bf16[128,128]{1,0:T(8,128)(2,1)S(1)}, bf16[128,128]{1,0:T(8,128)(2,1)}, u32[]{:S(2)}) %copy-start.5) | copy-done | bytes 32792
  7.2 0.0 copy-start.6
  7.2 0.7 %copy-done.6 = f32[4,128]{1,0:T(4,128)S(1)} copy-done((f32[4,128]{1,0:T(4,128)S(1)}, f32[4,128]{1,0:T(4,128)}, u32[]{:S(2)}) %copy-start.6) | copy-done | bytes 2072
  7.9 25.6 %shard_map.118 = (bf16[64,4096]{1,0:T(8,128)(2,1)S(1)}, bf16[128,512]{1,0:T(8,128)(2,1)S(1)}, bf16[128,512]{1,0:T(8,128)(2,1)S(1)}, f32[64,128]{1,0:T(8,128)S(1)...) custom-call(bf16[128,512]{1,0:T(8,128)(2,1)S(1)} %copy-done.2, bf16[128,512]{1,0:T(8,128)(2,1)S(1)} %copy-done.3, ...), custom_call_target="tpu_custom_call" | custom-call | flops 1073741824 | bytes 8388608 | tf_op jit(solution)/shard_map/pallas_call | solution.py:388
  33.5 0.8 %copy.19 = bf16[64,4096]{1,0:T(8,128)(2,1)} copy(bf16[64,4096]{1,0:T(8,128)(2,1)S(1)} %get-tuple-element.12) | data formatting | bytes 1048576
  34.3 0.7 %copy.20 = bf16[128,512]{1,0:T(8,128)(2,1)} copy(bf16[128,512]{1,0:T(8,128)(2,1)S(1)} %get-tuple-element.13) | data formatting | bytes 262144
  35.0 0.7 %copy.21 = bf16[128,512]{1,0:T(8,128)(2,1)} copy(bf16[128,512]{1,0:T(8,128)(2,1)S(1)} %get-tuple-element.14) | data formatting | bytes 262144
  35.6 0.6 %copy.22 = f32[64,128]{1,0:T(8,128)} copy(f32[64,128]{1,0:T(8,128)S(1)} %get-tuple-element.15) | data formatting | bytes 65536
  36.2 0.6 %copy.23 = f32[64,128]{1,0:T(8,128)} copy(f32[64,128]{1,0:T(8,128)S(1)} %get-tuple-element.16) | data formatting | bytes 65536
  36.9 0.6 %copy.24 = f32[4,128]{1,0:T(4,128)} copy(f32[4,128]{1,0:T(4,128)S(1)} %get-tuple-element.17) | data formatting | bytes 4096
Async XLA Ops:
  0.6 2.2 %copy-start = (bf16[512,4096]{1,0:T(8,128)(2,1)S(1)}, bf16[512,4096]{1,0:T(8,128)(2,1)}, u32[]{:S(2)}) copy-start(bf16[512,4096]{1,0:T(8,128)(2,1)} %w_hbm.1) | copy-start | bytes 12582916
  2.8 1.0 %copy-start.1 = (bf16[64,4096]{1,0:T(8,128)(2,1)S(1)}, bf16[64,4096]{1,0:T(8,128)(2,1)}, u32[]{:S(2)}) copy-start(bf16[64,4096]{1,0:T(8,128)(2,1)} %cot_hbm.1) | copy-start | bytes 1572868
  3.9 0.9 %copy-start.2 = (bf16[128,512]{1,0:T(8,128)(2,1)S(1)}, bf16[128,512]{1,0:T(8,128)(2,1)}, u32[]{:S(2)}) copy-start(bf16[128,512]{1,0:T(8,128)(2,1)} %x_hbm.1) | copy-start | bytes 393220
  4.8 0.9 %copy-start.3 = (bf16[128,512]{1,0:T(8,128)(2,1)S(1)}, bf16[128,512]{1,0:T(8,128)(2,1)}, u32[]{:S(2)}) copy-start(bf16[128,512]{1,0:T(8,128)(2,1)} %g_hbm.1) | copy-start | bytes 393220
  5.7 0.8 %copy-start.4 = (bf16[128,128]{1,0:T(8,128)(2,1)S(1)}, bf16[128,128]{1,0:T(8,128)(2,1)}, u32[]{:S(2)}) copy-start(bf16[128,128]{1,0:T(8,128)(2,1)} %b_hbm.1) | copy-start | bytes 98308
  6.4 0.8 %copy-start.5 = (bf16[128,128]{1,0:T(8,128)(2,1)S(1)}, bf16[128,128]{1,0:T(8,128)(2,1)}, u32[]{:S(2)}) copy-start(bf16[128,128]{1,0:T(8,128)(2,1)} %c_hbm.1) | copy-start | bytes 98308
  7.2 0.7 %copy-start.6 = (f32[4,128]{1,0:T(4,128)S(1)}, f32[4,128]{1,0:T(4,128)}, u32[]{:S(2)}) copy-start(f32[4,128]{1,0:T(4,128)} %ld_ref.1) | copy-start | bytes 6148

commit v2 on v1

--- a/solution.py
+++ b/solution.py
@@ -318,6 +318,18 @@
             @pl.when(ahead(k, d))
             def _():
                 z_copy(k, d).wait_send()
+
+
+def hand_over(*refs):
+    count = len(refs) // 2
+    sems = refs[-1]
+    copies = [
+        pltpu.make_async_copy(refs[i], refs[count + i], sems.at[i]) for i in range(count)
+    ]
+    for copy in copies:
+        copy.start()
+    for copy in copies:
+        copy.wait()
 
 
 def local(n_ctx, n_tp, inputs, gate_in, b_proj, c_proj, log_decay, w_out, cotangent):
@@ -385,7 +397,7 @@
     anywhere = pl.BlockSpec(memory_space=pl.ANY)
     vmem = pl.BlockSpec(memory_space=pltpu.VMEM)
     shape = jax.ShapeDtypeStruct
-    return pl.pallas_call(
+    results = pl.pallas_call(
         functools.partial(kernel, (inner, outer, n_tp, w_chunks, lo_chunks)),
         out_shape=(
             shape((rows, depth), BF16),
@@ -399,12 +411,21 @@
         out_specs=(vmem,) * 6,
         scratch_shapes=scratch,
         compiler_params=pltpu.CompilerParams(
-            collective_id=0, has_side_effects=True, vmem_limit_bytes=40 * 1024 * 1024
+            collective_id=0, has_side_effects=True, vmem_limit_bytes=56 * 1024 * 1024
         ),
         cost_estimate=pl.CostEstimate(
             flops=4 * BLOCK * width * depth, bytes_accessed=8 * 1024 * 1024, transcendentals=0
         ),
     )(inputs, gate_in, b_proj, c_proj, log_decay, w_out, cotangent)
+    return pl.pallas_call(
+        hand_over,
+        out_shape=[shape(r.shape, r.dtype) for r in results],
+        in_specs=[anywhere] * 6,
+        out_specs=(anywhere,) * 6,
+        scratch_shapes=[dma((6,))],
+        compiler_params=pltpu.CompilerParams(vmem_limit_bytes=56 * 1024 * 1024),
+        cost_estimate=pl.CostEstimate(flops=0, bytes_accessed=2 * 1024 * 1024, transcendentals=0),
+    )(*results)
 
 
 def solution(mesh):

time: 37.8 us -> 54.3 us (1.44)
  Pallas kernels: 25.6 us -> 53.5 us
  local copies, waits for them, and re-layouts: 11.1 us -> 0 us
    pallas_call x0 -> x1, Pallas kernels: none -> 27 us  [local(): pl.pallas_call(hand_over, out_shape=[shape(r.shape, r.dtype) for r in res...]
    unnamed x20 -> x0, local copies, waits for them, and re-layouts: 11.1 us -> none
    pallas_call x1, Pallas kernels: 25.6 us -> 26.5 us  [local(): pl.pallas_call(functools.partial(kernel, (inner, outer, n_tp, w_chunks, l...]
where the time goes in v2:
time: 54.3 us; the launch traced here: 54.1 us
  Pallas kernels  53.5 us (99%)
  between operations  0.64 us (1%)
    pallas_call x1, Pallas kernels, local(): pl.pallas_call(hand_over, out_shape=[shape(r.shape, r.dtype) for r in res...  27 us
    pallas_call x1, Pallas kernels, local(): pl.pallas_call(functools.partial(kernel, (inner, outer, n_tp, w_chunks, l...  26.5 us

profile of v2, /device:TPU:0, one launch (start us, length us, event | category | flops | bytes accessed | tf_op | source)
XLA Modules:
  0.0 54.1 jit_solution(9575424897121414928)
XLA Ops:
  0.6 26.5 %shard_map.118 = (bf16[64,4096]{1,0:T(8,128)(2,1)}, bf16[128,512]{1,0:T(8,128)(2,1)}, bf16[128,512]{1,0:T(8,128)(2,1)}, f32[64,128]{1,0:T(8,128)}, f32[64,128]{1,0:T(8,128)}, /*index=5*/f32[4,128]{1,0:T(4,128)}) custom-call(bf16[128,512]{1,0:T(8,128)(2,1)} %x_hbm.1, bf16[128,512]{1,0:T(8,128)(2,1)} %g_hbm.1, bf16[128,128]{1,0:T(8,128)(2,1)} %b_hbm.1, ...), custom_call_target="tpu_custom_call" | custom-call | flops 1073741824 | bytes 8388608 | tf_op jit(solution)/shard_map/pallas_call | solution.py:400
  27.1 27.0 %shard_map.119 = (bf16[64,4096]{1,0:T(8,128)(2,1)}, bf16[128,512]{1,0:T(8,128)(2,1)}, bf16[128,512]{1,0:T(8,128)(2,1)}, f32[64,128]{1,0:T(8,128)}, f32[64,128]{1,0:T(8,128)}, /*index=5*/f32[4,128]{1,0:T(4,128)}) custom-call(bf16[64,4096]{1,0:T(8,128)(2,1)} %get-tuple-element.12.refs_0_, bf16[128,512]{1,0:T(8,128)(2,1)} %get-tuple-element.13.refs_1_, ...), custom_call_target="tpu_custom_call" | custom-call | bytes 2097152 | tf_op jit(solution)/shard_map/pallas_call | solution.py:420
